TPU v7x, 512 devices: a whole 4x4x16 slice. The times are simulated.
512 devices in a mesh: seq: 32 (over z, core), item: 16 (over y, x).
Axes of the slice: x: 4, y: 4, z: 16, core: 2. Of those that a mesh axis runs over, the one named last changes fastest.
Arguments:
- history: bfloat16 [16, 4096, 512], P('item', 'seq'), may hold values from -6 to 6
- w_in: bfloat16 [512, 1536], replicated, may hold values from -0.25 to 0.25
- w_out: bfloat16 [512, 512], replicated, may hold values from -0.25 to 0.25
- item_table: bfloat16 [65536, 512], P(('seq', 'item')), may hold values from -6 to 6
- w_item_in: bfloat16 [512, 1024], replicated, may hold values from -0.25 to 0.25
- w_item_out: bfloat16 [1024, 512], replicated, may hold values from -0.1875 to 0.1875
- req_rows: int32 [16, 32, 512, 2], P('item', 'seq'), may hold values from 0 to 127
- req_counts: int32 [16, 32, 512], P('item', 'seq'), may hold values from 1 to 2, as said below
- labels: int32 [16, 4096, 4], P('item', 'seq'), may hold values from -1 to 1023, as said below
Outputs:
- position_loss: float32 [16, 4096], P('item', 'seq')
- item_table_gradient: float32 [65536, 512], P(('seq', 'item'))
Inputs may be any that keep to these rules, and one draw needn't show every extreme that they name: `req_rows`: slots at or beyond the block's count toward that owner are padding. `req_counts`: every history block uses all 2 slots toward some owner, and in every draw some owner is asked for 2 rows by every block. `labels`: A slot named is a used slot of the position's block; -1 names none; a slot may be named twice.
All inputs are finite; a program needn't handle non-finite values.
Results may differ from a plain program's by a relative error of at most 0.0085.
Values may be sent and summed in bfloat16 or wider, within the bound.
No kernel may reach another device: no remote copies, remote signals or barrier semaphores. Data moves between devices by JAX's collectives and lax.ppermute only.
A program may use at most 64 MiB of HBM per device.

v0:
```python
import jax
import jax.numpy as jnp
from jax import lax
from jax.experimental import pallas as pl
from jax.experimental.pallas import tpu as pltpu
from jax.sharding import Mesh
from jax.sharding import PartitionSpec as P

HEADS = 4
DQK = 64
TOK = 128
WIDTH = 512
HIDDEN = 1024
CHIPS = 16
HALF = CHIPS * TOK
TILE = 512
PACK_ROWS = 528
SEND_ROWS = 136
RANGE = 6.0
CODES = 32760.0

inverse_sharpness = 50.0
norm_eps = 1e-05
unit_eps = 1e-06

BF = jnp.bfloat16
F32 = jnp.float32
VMEM_LIMIT = 24 * 1024 * 1024
LARGE_LIMIT = 56 * 1024 * 1024

NN = (((1,), (0,)), ((), ()))
NT = (((1,), (1,)), ((), ()))


def dot(left, right, contract=NN):
    return lax.dot_general(left, right, contract, preferred_element_type=F32)


def half_silu(half):
    return half + half * jnp.tanh(half)


def silu(inputs):
    return half_silu(0.5 * inputs)


def split_product(left, weight):
    high = left.astype(BF)
    low = (left - high.astype(F32)).astype(BF)
    return dot(high, weight, NT) + dot(low, weight, NT)


def call(kernel, out_shape, inputs, scratch=(), limit=VMEM_LIMIT):
    return pl.pallas_call(
        kernel,
        out_shape=out_shape,
        in_specs=[pl.BlockSpec(memory_space=pltpu.VMEM)] * inputs,
        out_specs=jax.tree.map(lambda _: pl.BlockSpec(memory_space=pltpu.VMEM), out_shape),
        scratch_shapes=list(scratch),
        compiler_params=pltpu.CompilerParams(vmem_limit_bytes=limit),
    )


def prepare_kernel(
    history_ref, wanted_ref, counts_ref, labels_ref, table_ref, w_in_ref, w_out_ref,
    packed_ref, hidden_in_ref, raw_ref, copies_ref,
):
    rows = history_ref[...].astype(F32)
    root = jnp.exp(jnp.log(jnp.abs(rows) * (1.0 / RANGE)) * (1.0 / 3.0)) * CODES
    codes = jnp.where(rows < 0.0, -root, root)
    codes = jnp.round(codes).astype(jnp.int32).astype(jnp.int16)
    for part in range(4):
        packed_ref[part * TOK : (part + 1) * TOK, :] = codes[:, part * 128 : (part + 1) * 128]
    wanted = wanted_ref[...]
    slot = lax.broadcasted_iota(jnp.int32, (2, WIDTH), 0)
    wanted = jnp.where(slot < counts_ref[...], wanted, -1)
    extras = [
        wanted[slot : slot + 1, part * 128 : (part + 1) * 128] for slot in range(2) for part in range(4)
    ]
    extras += [labels_ref[...], jnp.zeros((4, TOK), jnp.int32)]
    packed_ref[WIDTH:PACK_ROWS, :] = jnp.concatenate(extras, axis=0).astype(jnp.int16)

    hidden_in = dot(table_ref[...], w_in_ref[...])
    hidden_in_ref[...] = hidden_in
    raw = dot(silu(hidden_in).astype(BF), w_out_ref[...])
    raw_ref[...] = raw
    inv_norm = lax.rsqrt(jnp.sum(raw * raw, axis=-1, keepdims=True) + unit_eps)
    embedding = (raw * inv_norm).astype(BF)
    for rank in range(32):
        copies_ref[rank] = embedding


def decode(codes):
    root = codes.astype(F32) * (RANGE ** (1.0 / 3.0) / CODES)
    return (root * root * root).astype(BF)


def rank_of(owner):
    return (owner % 16) * 2 + owner // 16


def label_places(labels_ref, block, entry, chip):
    label = labels_ref[block : block + 1, entry * TOK : (entry + 1) * TOK].astype(jnp.int32)
    local = label - chip * 64
    inside = (label >= 0) & (local >= 0) & (local < 64)
    return jnp.where(inside, (local & 1) * 32 + (local >> 1), -1)


def block_rows(packed_ref, chip, core):
    parts = [packed_ref[chip, core, part * TOK : (part + 1) * TOK, :] for part in range(4)]
    return jnp.concatenate(parts, axis=1)


def tower_kernel(
    packed_ref, w_in_ref, w_out_ref, user_ref, rows_ref, labels_ref,
    key_scr, value_scr, query_scr, total_scr,
):
    parity = lax.axis_index("core")
    chip = lax.axis_index("z")

    shift = TOK - lax.rem(chip, 4) * 32
    row_at = lax.broadcasted_iota(jnp.int32, (16, TOK), 0)
    chip_row = lax.div(chip, 4)
    for block in range(CHIPS):
        extras = packed_ref[block, parity, WIDTH:PACK_ROWS, :].astype(F32)
        mine = pltpu.roll(extras, shift, 1)
        for slot in range(2):
            chosen = jnp.where(row_at == chip_row + 4 * slot, mine, 0.0)
            at = slot * CHIPS + block
            rows_ref[at : at + 1, :] = jnp.sum(chosen, axis=0, keepdims=True)
        labels_ref[block : block + 1, :] = jnp.concatenate(
            [extras[8 + entry : 9 + entry] for entry in range(4)], axis=1
        )

    def project(step, carry):
        pieces = [block_rows(packed_ref, 2 * step + n // 2, n % 2) for n in range(4)]
        rows = decode(jnp.concatenate(pieces, axis=0))
        at = pl.ds(pl.multiple_of(step * TILE, TILE), TILE)
        value_scr[at, :] = silu(dot(rows, w_in_ref[:, 512:1024])).astype(BF)
        key_scr[:, at] = silu(dot(w_in_ref[:, 1280:1536], rows, (((0,), (1,)), ((), ())))).astype(BF)
        return carry

    lax.fori_loop(0, 2 * HALF // TILE, project, 0)

    lane = lax.broadcasted_iota(jnp.int32, (TILE, 2 * DQK), 1)

    def tile(top, height, start, width, diagonal=None):
        if diagonal is not None:
            row = lax.broadcasted_iota(jnp.int32, (height, width), 0)
            key_at = lax.broadcasted_iota(jnp.int32, (height, width), 1) + diagonal[0]
            block = row // TOK + diagonal[1]
            allowed = key_at <= (2 * block + parity) * TOK + row % TOK
        weights = []
        for head in range(HEADS):
            keys = key_scr[(head // 2) * 2 * DQK : (head // 2 + 1) * 2 * DQK, pl.ds(start, width)]
            weight = half_silu(dot(query_scr[head, top : top + height], keys))
            if diagonal is not None:
                weight = jnp.where(allowed, weight, 0.0)
            weights.append(weight.astype(BF))
        for head in range(HEADS):
            values = value_scr[pl.ds(start, width), head * 128 : (head + 1) * 128]
            total_scr[top : top + height, head * 128 : (head + 1) * 128] += dot(weights[head], values)

    for group in range(HALF // TILE):
        rows = decode(
            jnp.concatenate([block_rows(packed_ref, 4 * group + n, parity) for n in range(4)], axis=0)
        )
        query = (silu(dot(rows, w_in_ref[:, 1024:1280])).astype(BF) * 0.0625).astype(BF)
        for head in range(HEADS):
            both = query[:, (head // 2) * 2 * DQK : (head // 2 + 1) * 2 * DQK]
            mine = (lane >= DQK) if head % 2 else (lane < DQK)
            query_scr[head] = jnp.where(mine, both, jnp.zeros_like(both))
        total_scr[...] = jnp.zeros_like(total_scr)
        base = group * 2 * TILE

        def earlier(step, carry):
            tile(0, TILE, pl.multiple_of(step * TILE, TILE), TILE)
            return carry

        lax.fori_loop(0, base // TILE, earlier, 0)
        for pair in range(2):
            top = pair * 2 * TOK
            first = base + 2 * top
            if pair:
                tile(top, 2 * TOK, base, TILE)
            tile(top, 2 * TOK, first, 2 * TOK, (0, 0))
            tile(top + TOK, TOK, first + 2 * TOK, 2 * TOK, (2 * TOK, 1))

        attended = total_scr[...]
        centered = attended - jnp.mean(attended, axis=-1, keepdims=True)
        variance = jnp.mean(centered * centered, axis=-1, keepdims=True)
        normed = centered * lax.rsqrt(variance + norm_eps)
        gate_units = silu(dot(rows, w_in_ref[:, 0:512]))
        mixed_rows = (normed * gate_units).astype(BF)
        updated = rows.astype(F32) + dot(mixed_rows, w_out_ref[...])
        scale = lax.rsqrt(jnp.sum(updated * updated, axis=-1, keepdims=True) + unit_eps)
        user_ref[group * TILE : (group + 1) * TILE, :] = (updated * scale).astype(BF)


def scores_kernel(
    table_ref, user_ref, rows_ref, labels_ref, exps_ref, hits_ref, exchange_ref, entry_scr
):
    chip = lax.axis_index("z")
    row_ids = lax.broadcasted_iota(jnp.int32, (32, TOK), 1).astype(F32)
    for owner in range(32):
        asked = jnp.broadcast_to(rows_ref[:, owner : owner + 1], (32, TOK))
        rows = dot((row_ids == asked).astype(BF), table_ref[rank_of(owner)])
        used = (asked >= 0.0).astype(F32)
        for slot in range(2):
            entry_scr[4, pl.ds(slot * 32 + owner, 16, stride=64), :] = used[
                slot * 16 : (slot + 1) * 16
            ]
            for part in range(4):
                entry_scr[part, pl.ds(slot * 32 + owner, 16, stride=64), :] = rows[
                    slot * 16 : (slot + 1) * 16, part * 128 : (part + 1) * 128
                ]
    slot_ids = lax.broadcasted_iota(jnp.int32, (64, TOK), 0)
    exchange_ref[...] = jnp.zeros_like(exchange_ref)
    for block in range(CHIPS):
        entries = jnp.concatenate(
            [entry_scr[part, block * 64 : (block + 1) * 64, :] for part in range(4)], axis=1
        ).astype(BF)
        scores = dot(entries, user_ref[block * TOK : (block + 1) * TOK, :], NT) * inverse_sharpness
        used = entry_scr[4, block * 64 : (block + 1) * 64, :] > 0.0
        exps = jnp.where(used, jnp.exp(scores), 0.0)
        exps_ref[block] = exps
        hits = jnp.zeros((64, TOK), F32)
        for entry in range(4):
            place = label_places(labels_ref, block, entry, chip)
            hits = hits + (slot_ids == place).astype(F32)
        hits_ref[block] = hits
        total = jnp.sum(exps, axis=0, keepdims=True)
        exchange_ref[:, block : block + 1, :] = jnp.broadcast_to(total[None], (CHIPS, 1, TOK))
        exchange_ref[block, 16:17, :] = jnp.sum(hits * scores, axis=0, keepdims=True)


def gradient_kernel(
    exps_ref, hits_ref, user_ref, exchange_ref, labels_ref, rows_ref,
    send_ref, loss_ref, grad_scr,
):
    chip = lax.axis_index("z")
    sums = jnp.sum(exchange_ref[...], axis=0)
    positives = jnp.zeros((CHIPS, TOK), F32)
    for entry in range(4):
        positives = positives + (labels_ref[:, entry * TOK : (entry + 1) * TOK] >= 0.0).astype(F32)
    divisor = jnp.maximum(positives, 1.0)
    totals = sums[0:16]
    own = lax.broadcasted_iota(jnp.int32, (CHIPS, TOK), 0) == chip
    losses = (positives * jnp.log(totals) - sums[16:17]) / divisor
    loss_ref[...] = jnp.sum(jnp.where(own, losses, 0.0), axis=0, keepdims=True)
    exp_scale = positives / (divisor * totals)
    hit_scale = 1.0 / divisor
    for block in range(CHIPS):
        score_grad = (
            exps_ref[block] * exp_scale[block : block + 1]
            - hits_ref[block] * hit_scale[block : block + 1]
        ).astype(BF)
        grads = dot(score_grad, user_ref[block * TOK : (block + 1) * TOK, :]) * inverse_sharpness
        for slot in range(2):
            for part in range(4):
                for side in range(2):
                    at = side * SEND_ROWS + part * 32 + slot * 16 + block
                    first = slot * 32 + side * 16
                    grad_scr[pl.ds(at, 16, stride=2 * SEND_ROWS), :] = grads[
                        first : first + 16, part * 128 : (part + 1) * 128
                    ]
    sender = lax.axis_index("item") * 2 + lax.axis_index("core")
    at = lax.broadcasted_iota(jnp.int32, (32, TOK), 0) + (sender & 3) * 32
    spread = (lax.broadcasted_iota(jnp.int32, (32, TOK), 1) == at).astype(BF)
    index = dot(rows_ref[...].astype(BF), spread, (((0,), (0,)), ((), ())))[0:32]
    zeros = jnp.zeros((16, TOK), F32)
    for side in range(2):
        for extra in range(SEND_ROWS - TOK):
            rows = zeros if extra else index[side * 16 : (side + 1) * 16]
            grad_scr[pl.ds(side * SEND_ROWS + TOK + extra, 16, stride=2 * SEND_ROWS), :] = rows
    send_ref[...] = grad_scr[...].astype(BF)


def owner_kernel(
    arrived_ref, index_ref, hidden_in_ref, raw_ref, w_in_ref, w_out_ref, gradient_ref, rows_scr
):
    row_ids = lax.broadcasted_iota(jnp.int32, (TOK, TOK), 0).astype(F32)
    row_grad = jnp.zeros((TOK, WIDTH), F32)
    for group in range(8):
        index = jnp.zeros((1, TOK), F32)
        for member in range(4):
            sender = group * 4 + member
            index = index + index_ref[sender : sender + 1, :]
            for part in range(4):
                rows_scr[member * 32 : (member + 1) * 32, part * 128 : (part + 1) * 128] = arrived_ref[
                    sender, part * 32 : (part + 1) * 32, :
                ]
        pick = (row_ids == index).astype(BF)
        row_grad = row_grad + dot(pick, rows_scr[...])
    raw = raw_ref[...]
    inv_norm = lax.rsqrt(jnp.sum(raw * raw, axis=-1, keepdims=True) + unit_eps)
    unit = raw * inv_norm
    raw_grad = (row_grad - unit * jnp.sum(unit * row_grad, axis=-1, keepdims=True)) * inv_norm
    hidden_grad = split_product(raw_grad, w_out_ref[...])
    hidden_in = hidden_in_ref[...]
    sigma = 0.5 * jnp.tanh(0.5 * hidden_in) + 0.5
    input_grad = hidden_grad * (sigma * (1.0 + hidden_in * (1.0 - sigma)))
    gradient_ref[...] = split_product(input_grad, w_in_ref[...])


def on_device(
    history, w_in, w_out, item_table, w_item_in, w_item_out, req_rows, req_counts, labels
):
    with jax.named_scope("prepare"):
        packed, hidden_in, raw_embed, copies = call(
            prepare_kernel,
            (
                jax.ShapeDtypeStruct((PACK_ROWS, 128), jnp.int16),
                jax.ShapeDtypeStruct((TOK, HIDDEN), F32),
                jax.ShapeDtypeStruct((TOK, WIDTH), F32),
                jax.ShapeDtypeStruct((32, TOK, WIDTH), BF),
            ),
            7,
            limit=LARGE_LIMIT,
        )(
            history[0], req_rows[0, 0].T, req_counts[0], labels[0].T,
            item_table, w_item_in, w_item_out,
        )

    with jax.named_scope("table_copies"):
        table = lax.all_to_all(copies, ("item", "core"), split_axis=0, concat_axis=0, tiled=True)

    with jax.named_scope("history_gather"):
        gathered = lax.all_gather(packed, ("z", "core"), axis=0, tiled=True)

    with jax.named_scope("tower"):
        user_rows, asked_rows, label_rows = call(
            tower_kernel,
            (
                jax.ShapeDtypeStruct((HALF, WIDTH), BF),
                jax.ShapeDtypeStruct((32, TOK), F32),
                jax.ShapeDtypeStruct((CHIPS, WIDTH), F32),
            ),
            3,
            [
                pltpu.VMEM((HEADS * DQK, 2 * HALF), BF),
                pltpu.VMEM((2 * HALF, WIDTH), BF),
                pltpu.VMEM((HEADS, TILE, 2 * DQK), BF),
                pltpu.VMEM((TILE, WIDTH), F32),
            ],
        )(gathered.reshape(CHIPS, 2, PACK_ROWS, 128), w_in, w_out)

    with jax.named_scope("scores"):
        exps, hits, exchange = call(
            scores_kernel,
            (
                jax.ShapeDtypeStruct((CHIPS, 64, TOK), F32),
                jax.ShapeDtypeStruct((CHIPS, 64, TOK), F32),
                jax.ShapeDtypeStruct((CHIPS, 24, TOK), F32),
            ),
            4,
            [pltpu.VMEM((5, 1024, 128), F32)],
        )(table, user_rows, asked_rows, label_rows)

    with jax.named_scope("totals_exchange"):
        exchange = lax.all_to_all(exchange, "z", split_axis=0, concat_axis=0, tiled=True)

    with jax.named_scope("gradient_rows"):
        send, loss = call(
            gradient_kernel,
            (
                jax.ShapeDtypeStruct((32 * SEND_ROWS, 128), BF),
                jax.ShapeDtypeStruct((1, TOK), F32),
            ),
            6,
            [pltpu.VMEM((32 * SEND_ROWS, 128), F32)],
        )(exps, hits, user_rows, exchange, label_rows, asked_rows)

    with jax.named_scope("gradient_send"):
        arrived = lax.all_to_all(
            send.reshape(32, SEND_ROWS, 128), ("item", "core"), split_axis=0, concat_axis=0, tiled=True
        )

    with jax.named_scope("owner"):
        gradient = call(
            owner_kernel,
            jax.ShapeDtypeStruct((TOK, WIDTH), F32),
            6,
            [pltpu.VMEM((TOK, WIDTH), BF)],
        )(arrived, arrived[:, TOK].astype(F32), hidden_in, raw_embed, w_item_in, w_item_out)
    return (loss, gradient)


def solution(mesh):
    split = Mesh(mesh.devices.reshape(CHIPS, 2, 16), ("z", "core", "item"))
    rows = ("z", "core")
    placed = (
        P("item", rows, None),
        P(),
        P(),
        P(("z", "core", "item"), None),
        P(),
        P(),
        P("item", rows, None, None),
        P("item", rows, None),
        P("item", rows, None),
    )
    return jax.shard_map(
        on_device,
        mesh=split,
        in_specs=placed,
        out_specs=(P("item", rows), P(("z", "core", "item"), None)),
        check_vma=False,
    )
```

profile of v0, /device:TPU:1, one launch (start us, length us, event | category | flops | bytes accessed | tf_op | source)
XLA Modules:
  0.0 154.8 jit_solution(15783746385248761823)
XLA Ops:
  0.6 4.6 %prepare.1 = (s16[528,128]{1,0:T(8,128)(2,1)}, f32[128,1024]{1,0:T(8,128)}, f32[128,512]{1,0:T(8,128)}, bf16[32,128,512]{2,1,0:T(8,128)(2,1)}) custom-call(bf16[128,512]{1,0:T(8,128)(2,1)} %bitcast.17, s32[2,512]{1,0:T(2,128)} %bitcast.18, s32[1,512]{1,0:T(1,128)} %bitcast.19, s32[4,128]{1,0:T(4,128)} %bitcast.20, bf16[128,512]{1,0:T(8,128)(2,1)} %table_ref.1, ...), custom_call_target="tpu_custom_call" | custom-call | tf_op jit(solution)/shard_map/prepare/pallas_call | solution.py:310
  5.3 0.0 copy-start.6
  5.3 11.5 %all-to-all-start = ((bf16[32,128,512]{2,1,0:T(8,128)(2,1)}), bf16[32,128,512]{2,1,0:T(8,128)(2,1)}, u32[]{:S(2)}, u32[]{:S(2)}) async-start(bf16[32,128,512]{2,1,0:T(8,128)(2,1)} %get-tuple-element.14), calls=%async_computation | async-start | bytes 8388608 | tf_op jit(solution)/shard_map/table_copies/all_to_all | solution.py:326
  16.7 0.0 copy-done.6
  16.7 0.0 copy-start.2
  16.8 0.0 copy-start.3
  16.8 47.7 %all-gather.1 = s16[16896,128]{1,0:T(8,128)(2,1)S(1)} all-gather(s16[528,128]{1,0:T(8,128)(2,1)S(1)} %copy-done.6), channel_id=1, replica_groups=mesh['z'=16,'core'=2,'item'=16] {'z','core'}, dimensions={0}, use_global_device_ids=true | all-gather | bytes 4460544 | tf_op jit(solution)/shard_map/history_gather/all_gather | solution.py:329
  64.5 0.0 copy-done.2
  64.5 0.0 copy-done.3
  64.5 31.7 %tower.1 = (bf16[2048,512]{1,0:T(8,128)(2,1)S(1)}, f32[32,128]{1,0:T(8,128)S(1)}, f32[16,512]{1,0:T(8,128)S(1)}) custom-call(s16[16,2,528,128]{3,2,1,0:T(8,128)(2,1)S(1)} %bitcast.15, bf16[512,1536]{1,0:T(8,128)(2,1)S(1)} %copy-done.2, bf16[512,512]{1,0:T(8,128)(2,1)S(1)} %copy-done.3), custom_call_target="tpu_custom_call" | custom-call | tf_op jit(solution)/shard_map/tower/pallas_call | solution.py:332
  96.2 0.0 all-to-all-done.table_ref
  96.2 6.0 %scores.1 = (f32[16,64,128]{2,1,0:T(8,128)S(1)}, f32[16,64,128]{2,1,0:T(8,128)S(1)}, f32[16,24,128]{2,1,0:T(8,128)S(1)}) custom-call(bf16[32,128,512]{2,1,0:T(8,128)(2,1)} %all-to-all-done.table_ref, bf16[2048,512]{1,0:T(8,128)(2,1)S(1)} %get-tuple-element.16.user_ref, f32[32,128]{1,0:T(8,128)S(1)} %get-tuple-element.17.rows_ref, ...), custom_call_target="tpu_custom_call" | custom-call | tf_op jit(solution)/shard_map/scores/pallas_call | solution.py:349
  102.2 19.6 %all_to_all.15.exchange_ref = f32[16,24,128]{2,1,0:T(8,128)S(1)} all-to-all(f32[16,24,128]{2,1,0:T(8,128)S(1)} %get-tuple-element.21), channel_id=1, replica_groups=mesh['z'=16,'core'=2,'item'=16] {'z'}, dimensions={0} | all-to-all | bytes 393216 | tf_op jit(solution)/shard_map/totals_exchange/all_to_all | solution.py:361
  121.7 0.0 copy-start
  121.7 0.0 copy-start.1
  121.7 0.0 copy-start.4
  121.7 0.0 copy-start.5
  121.8 1.8 %gradient_rows.1 = (bf16[4352,128]{1,0:T(8,128)(2,1)S(1)}, f32[1,128]{1,0:T(1,128)}) custom-call(f32[16,64,128]{2,1,0:T(8,128)S(1)} %get-tuple-element.19.exps_ref, f32[16,64,128]{2,1,0:T(8,128)S(1)} %get-tuple-element.20.hits_ref, bf16[2048,512]{1,0:T(8,128)(2,1)S(1)} %get-tuple-element.16.user_ref, f32[16,24,128]{2,1,0:T(8,128)S(1)} %all_to_all.15.exchange_ref, ...), custom_call_target="tpu_custom_call" | custom-call | tf_op jit(solution)/shard_map/gradient_rows/pallas_call | solution.py:364
  123.6 28.4 %all_to_all.16.arrived_ref = bf16[32,136,128]{2,1,0:T(8,128)(2,1)S(1)} all-to-all(bf16[32,136,128]{2,1,0:T(8,128)(2,1)S(1)} %bitcast.16), channel_id=1, replica_groups=mesh['z'=16,'core'=2,'item'=16] {'item','core'}, dimensions={0} | all-to-all | bytes 2228224 | tf_op jit(solution)/shard_map/gradient_send/all_to_all | solution.py:375
  152.0 0.0 copy-done
  152.0 0.0 copy-done.1
  152.0 0.0 copy-done.4
  152.0 0.0 copy-done.5
  152.0 2.8 %owner.1 = f32[128,512]{1,0:T(8,128)} custom-call(bf16[32,136,128]{2,1,0:T(8,128)(2,1)S(1)} %all_to_all.16.arrived_ref, f32[32,128]{1,0:T(8,128)S(1)} %fusion.index_ref, f32[128,1024]{1,0:T(8,128)S(1)} %copy-done.4, f32[128,512]{1,0:T(8,128)S(1)} %copy-done.5, bf16[512,1024]{1,0:T(8,128)(2,1)S(1)} %copy-done, bf16[1024,512]{1,0:T(8,128)(2,1)S(1)} %copy-done.1), custom_call_target="tpu_custom_call" | custom-call | tf_op jit(solution)/shard_map/owner/pallas_call | solution.py:380
  (2 shorter events, 0.0 us)
Async XLA Ops:
  5.3 11.5 %copy-start.6 = (s16[528,128]{1,0:T(8,128)(2,1)S(1)}, s16[528,128]{1,0:T(8,128)(2,1)}, u32[]{:S(2)}) copy-start(s16[528,128]{1,0:T(8,128)(2,1)} %get-tuple-element.15) | copy-start | bytes 405508
  5.3 90.9 %all-to-all-start = ((bf16[32,128,512]{2,1,0:T(8,128)(2,1)}), bf16[32,128,512]{2,1,0:T(8,128)(2,1)}, u32[]{:S(2)}, u32[]{:S(2)}) async-start(bf16[32,128,512]{2,1,0:T(8,128)(2,1)} %get-tuple-element.14), calls=%async_computation | async-start | bytes 8388608 | tf_op jit(solution)/shard_map/table_copies/all_to_all | solution.py:326
  16.7 47.8 %copy-start.2 = (bf16[512,1536]{1,0:T(8,128)(2,1)S(1)}, bf16[512,1536]{1,0:T(8,128)(2,1)}, u32[]{:S(2)}) copy-start(bf16[512,1536]{1,0:T(8,128)(2,1)} %w_in_ref.4) | copy-start | bytes 4718596
  16.8 47.8 %copy-start.3 = (bf16[512,512]{1,0:T(8,128)(2,1)S(1)}, bf16[512,512]{1,0:T(8,128)(2,1)}, u32[]{:S(2)}) copy-start(bf16[512,512]{1,0:T(8,128)(2,1)} %w_out_ref.4) | copy-start | bytes 1572868
  121.7 30.2 %copy-start = (bf16[512,1024]{1,0:T(8,128)(2,1)S(1)}, bf16[512,1024]{1,0:T(8,128)(2,1)}, u32[]{:S(2)}) copy-start(bf16[512,1024]{1,0:T(8,128)(2,1)} %w_in_ref.5) | copy-start | bytes 3145732
  121.7 30.2 %copy-start.1 = (bf16[1024,512]{1,0:T(8,128)(2,1)S(1)}, bf16[1024,512]{1,0:T(8,128)(2,1)}, u32[]{:S(2)}) copy-start(bf16[1024,512]{1,0:T(8,128)(2,1)} %w_out_ref.5) | copy-start | bytes 3145732
  121.7 30.3 %copy-start.4 = (f32[128,1024]{1,0:T(8,128)S(1)}, f32[128,1024]{1,0:T(8,128)}, u32[]{:S(2)}) copy-start(f32[128,1024]{1,0:T(8,128)} %get-tuple-element.24.hidden_in_ref) | copy-start | bytes 1572868
  121.7 30.3 %copy-start.5 = (f32[128,512]{1,0:T(8,128)S(1)}, f32[128,512]{1,0:T(8,128)}, u32[]{:S(2)}) copy-start(f32[128,512]{1,0:T(8,128)} %get-tuple-element.25.raw_ref) | copy-start | bytes 786436
where the time goes:
time: 155 us
  blocking collectives  95.7 us (62%)
  Pallas kernels  46.9 us (30%)
  starting transfers between devices  11.5 us (7%)
    all_gather x1, blocking collectives, on_device(): gathered = lax.all_gather(packed, ('z', 'core'), axis=0, tiled=True)  47.7 us
    pallas_call x1, Pallas kernels, on_device(): call(tower_kernel, (jax.ShapeDtypeStruct((HALF, WIDTH), BF), jax.ShapeDty...  31.7 us
    all_to_all x1, blocking collectives, on_device(): lax.all_to_all(send.reshape(32, SEND_ROWS, 128), ('item', 'core'), split_...  28.4 us
    all_to_all x1, blocking collectives, on_device(): lax.all_to_all(exchange, 'z', split_axis=0, concat_axis=0, tiled=True)  19.6 us
    all_to_all x1, starting transfers between devices, on_device(): lax.all_to_all(copies, ('item', 'core'), split_axis=0, concat_axis=0, til...  11.5 us
    pallas_call x1, Pallas kernels, on_device(): call(scores_kernel, (jax.ShapeDtypeStruct((CHIPS, 64, TOK), F32), jax.Sha...  5.95 us
    pallas_call x1, Pallas kernels, on_device(): call(prepare_kernel, (jax.ShapeDtypeStruct((PACK_ROWS, 128), jnp.int16),...  4.64 us
  transfers between devices with their start and end apart: 1, of which 0 were waited for; matrix products, arithmetic and copies ran while one was open for 0% of the time, Pallas kernels for 20%

commit v1 on v0

--- a/solution.py
+++ b/solution.py
@@ -27,6 +27,7 @@
 F32 = jnp.float32
 VMEM_LIMIT = 24 * 1024 * 1024
 LARGE_LIMIT = 56 * 1024 * 1024
+TOWER_LIMIT = 32 * 1024 * 1024
 
 NN = (((1,), (0,)), ((), ()))
 NT = (((1,), (1,)), ((), ()))
@@ -174,10 +175,10 @@
         base = group * 2 * TILE
 
         def earlier(step, carry):
-            tile(0, TILE, pl.multiple_of(step * TILE, TILE), TILE)
+            tile(0, TILE, pl.multiple_of(step * 2 * TILE, 2 * TILE), 2 * TILE)
             return carry
 
-        lax.fori_loop(0, base // TILE, earlier, 0)
+        lax.fori_loop(0, group, earlier, 0)
         for pair in range(2):
             top = pair * 2 * TOK
             first = base + 2 * top
@@ -343,6 +344,7 @@
                 pltpu.VMEM((HEADS, TILE, 2 * DQK), BF),
                 pltpu.VMEM((TILE, WIDTH), F32),
             ],
+            limit=TOWER_LIMIT,
         )(gathered.reshape(CHIPS, 2, PACK_ROWS, 128), w_in, w_out)
 
     with jax.named_scope("scores"):

time: 155 us -> 154 us (level)
  no operation moved by 1% of the time
where the time goes in v1:
time: 154 us
  blocking collectives  95.7 us (62%)
  Pallas kernels  45.7 us (30%)
  starting transfers between devices  11.5 us (7%)
    all_gather x1, blocking collectives, on_device(): gathered = lax.all_gather(packed, ('z', 'core'), axis=0, tiled=True)  47.7 us
    pallas_call x1, Pallas kernels, on_device(): call(tower_kernel, (jax.ShapeDtypeStruct((HALF, WIDTH), BF), jax.ShapeDty...  30.5 us
    all_to_all x1, blocking collectives, on_device(): lax.all_to_all(send.reshape(32, SEND_ROWS, 128), ('item', 'core'), split_...  28.4 us
    all_to_all x1, blocking collectives, on_device(): lax.all_to_all(exchange, 'z', split_axis=0, concat_axis=0, tiled=True)  19.6 us
    all_to_all x1, starting transfers between devices, on_device(): lax.all_to_all(copies, ('item', 'core'), split_axis=0, concat_axis=0, til...  11.5 us
    pallas_call x1, Pallas kernels, on_device(): call(scores_kernel, (jax.ShapeDtypeStruct((CHIPS, 64, TOK), F32), jax.Sha...  5.95 us
    pallas_call x1, Pallas kernels, on_device(): call(prepare_kernel, (jax.ShapeDtypeStruct((PACK_ROWS, 128), jnp.int16),...  4.64 us
  transfers between devices with their start and end apart: 1, of which 0 were waited for; matrix products, arithmetic and copies ran while one was open for 0% of the time, Pallas kernels for 20%

profile of v1, /device:TPU:1, one launch (start us, length us, event | category | flops | bytes accessed | tf_op | source)
XLA Modules:
  0.0 153.6 jit_solution(3903656174747273933)
XLA Ops:
  0.6 4.6 %prepare.1 = (s16[528,128]{1,0:T(8,128)(2,1)}, f32[128,1024]{1,0:T(8,128)}, f32[128,512]{1,0:T(8,128)}, bf16[32,128,512]{2,1,0:T(8,128)(2,1)}) custom-call(bf16[128,512]{1,0:T(8,128)(2,1)} %bitcast.17, s32[2,512]{1,0:T(2,128)} %bitcast.18, s32[1,512]{1,0:T(1,128)} %bitcast.19, s32[4,128]{1,0:T(4,128)} %bitcast.20, bf16[128,512]{1,0:T(8,128)(2,1)} %table_ref.1, ...), custom_call_target="tpu_custom_call" | custom-call | tf_op jit(solution)/shard_map/prepare/pallas_call | solution.py:311
  5.3 0.0 copy-start.6
  5.3 11.5 %all-to-all-start = ((bf16[32,128,512]{2,1,0:T(8,128)(2,1)}), bf16[32,128,512]{2,1,0:T(8,128)(2,1)}, u32[]{:S(2)}, u32[]{:S(2)}) async-start(bf16[32,128,512]{2,1,0:T(8,128)(2,1)} %get-tuple-element.14), calls=%async_computation | async-start | bytes 8388608 | tf_op jit(solution)/shard_map/table_copies/all_to_all | solution.py:327
  16.7 0.0 copy-done.6
  16.7 0.0 copy-start.2
  16.8 0.0 copy-start.3
  16.8 47.7 %all-gather.1 = s16[16896,128]{1,0:T(8,128)(2,1)S(1)} all-gather(s16[528,128]{1,0:T(8,128)(2,1)S(1)} %copy-done.6), channel_id=1, replica_groups=mesh['z'=16,'core'=2,'item'=16] {'z','core'}, dimensions={0}, use_global_device_ids=true | all-gather | bytes 4460544 | tf_op jit(solution)/shard_map/history_gather/all_gather | solution.py:330
  64.5 0.0 copy-done.2
  64.5 0.0 copy-done.3
  64.5 30.5 %tower.1 = (bf16[2048,512]{1,0:T(8,128)(2,1)S(1)}, f32[32,128]{1,0:T(8,128)S(1)}, f32[16,512]{1,0:T(8,128)S(1)}) custom-call(s16[16,2,528,128]{3,2,1,0:T(8,128)(2,1)S(1)} %bitcast.15, bf16[512,1536]{1,0:T(8,128)(2,1)S(1)} %copy-done.2, bf16[512,512]{1,0:T(8,128)(2,1)S(1)} %copy-done.3), custom_call_target="tpu_custom_call" | custom-call | tf_op jit(solution)/shard_map/tower/pallas_call | solution.py:333
  95.0 0.0 all-to-all-done.table_ref
  95.0 6.0 %scores.1 = (f32[16,64,128]{2,1,0:T(8,128)S(1)}, f32[16,64,128]{2,1,0:T(8,128)S(1)}, f32[16,24,128]{2,1,0:T(8,128)S(1)}) custom-call(bf16[32,128,512]{2,1,0:T(8,128)(2,1)} %all-to-all-done.table_ref, bf16[2048,512]{1,0:T(8,128)(2,1)S(1)} %get-tuple-element.16.user_ref, f32[32,128]{1,0:T(8,128)S(1)} %get-tuple-element.17.rows_ref, ...), custom_call_target="tpu_custom_call" | custom-call | tf_op jit(solution)/shard_map/scores/pallas_call | solution.py:351
  101.0 19.6 %all_to_all.15.exchange_ref = f32[16,24,128]{2,1,0:T(8,128)S(1)} all-to-all(f32[16,24,128]{2,1,0:T(8,128)S(1)} %get-tuple-element.21), channel_id=1, replica_groups=mesh['z'=16,'core'=2,'item'=16] {'z'}, dimensions={0} | all-to-all | bytes 393216 | tf_op jit(solution)/shard_map/totals_exchange/all_to_all | solution.py:363
  120.6 0.0 copy-start
  120.6 0.0 copy-start.1
  120.6 0.0 copy-start.4
  120.6 0.0 copy-start.5
  120.6 1.8 %gradient_rows.1 = (bf16[4352,128]{1,0:T(8,128)(2,1)S(1)}, f32[1,128]{1,0:T(1,128)}) custom-call(f32[16,64,128]{2,1,0:T(8,128)S(1)} %get-tuple-element.19.exps_ref, f32[16,64,128]{2,1,0:T(8,128)S(1)} %get-tuple-element.20.hits_ref, bf16[2048,512]{1,0:T(8,128)(2,1)S(1)} %get-tuple-element.16.user_ref, f32[16,24,128]{2,1,0:T(8,128)S(1)} %all_to_all.15.exchange_ref, ...), custom_call_target="tpu_custom_call" | custom-call | tf_op jit(solution)/shard_map/gradient_rows/pallas_call | solution.py:366
  122.4 28.4 %all_to_all.16.arrived_ref = bf16[32,136,128]{2,1,0:T(8,128)(2,1)S(1)} all-to-all(bf16[32,136,128]{2,1,0:T(8,128)(2,1)S(1)} %bitcast.16), channel_id=1, replica_groups=mesh['z'=16,'core'=2,'item'=16] {'item','core'}, dimensions={0} | all-to-all | bytes 2228224 | tf_op jit(solution)/shard_map/gradient_send/all_to_all | solution.py:377
  150.8 0.0 copy-done
  150.8 0.0 copy-done.1
  150.8 0.0 copy-done.4
  150.8 0.0 copy-done.5
  150.8 2.8 %owner.1 = f32[128,512]{1,0:T(8,128)} custom-call(bf16[32,136,128]{2,1,0:T(8,128)(2,1)S(1)} %all_to_all.16.arrived_ref, f32[32,128]{1,0:T(8,128)S(1)} %fusion.index_ref, f32[128,1024]{1,0:T(8,128)S(1)} %copy-done.4, f32[128,512]{1,0:T(8,128)S(1)} %copy-done.5, bf16[512,1024]{1,0:T(8,128)(2,1)S(1)} %copy-done, bf16[1024,512]{1,0:T(8,128)(2,1)S(1)} %copy-done.1), custom_call_target="tpu_custom_call" | custom-call | tf_op jit(solution)/shard_map/owner/pallas_call | solution.py:382
  (2 shorter events, 0.0 us)
Async XLA Ops:
  5.3 11.5 %copy-start.6 = (s16[528,128]{1,0:T(8,128)(2,1)S(1)}, s16[528,128]{1,0:T(8,128)(2,1)}, u32[]{:S(2)}) copy-start(s16[528,128]{1,0:T(8,128)(2,1)} %get-tuple-element.15) | copy-start | bytes 405508
  5.3 89.7 %all-to-all-start = ((bf16[32,128,512]{2,1,0:T(8,128)(2,1)}), bf16[32,128,512]{2,1,0:T(8,128)(2,1)}, u32[]{:S(2)}, u32[]{:S(2)}) async-start(bf16[32,128,512]{2,1,0:T(8,128)(2,1)} %get-tuple-element.14), calls=%async_computation | async-start | bytes 8388608 | tf_op jit(solution)/shard_map/table_copies/all_to_all | solution.py:327
  16.7 47.8 %copy-start.2 = (bf16[512,1536]{1,0:T(8,128)(2,1)S(1)}, bf16[512,1536]{1,0:T(8,128)(2,1)}, u32[]{:S(2)}) copy-start(bf16[512,1536]{1,0:T(8,128)(2,1)} %w_in_ref.4) | copy-start | bytes 4718596
  16.8 47.8 %copy-start.3 = (bf16[512,512]{1,0:T(8,128)(2,1)S(1)}, bf16[512,512]{1,0:T(8,128)(2,1)}, u32[]{:S(2)}) copy-start(bf16[512,512]{1,0:T(8,128)(2,1)} %w_out_ref.4) | copy-start | bytes 1572868
  120.6 30.2 %copy-start = (bf16[512,1024]{1,0:T(8,128)(2,1)S(1)}, bf16[512,1024]{1,0:T(8,128)(2,1)}, u32[]{:S(2)}) copy-start(bf16[512,1024]{1,0:T(8,128)(2,1)} %w_in_ref.5) | copy-start | bytes 3145732
  120.6 30.2 %copy-start.1 = (bf16[1024,512]{1,0:T(8,128)(2,1)S(1)}, bf16[1024,512]{1,0:T(8,128)(2,1)}, u32[]{:S(2)}) copy-start(bf16[1024,512]{1,0:T(8,128)(2,1)} %w_out_ref.5) | copy-start | bytes 3145732
  120.6 30.2 %copy-start.4 = (f32[128,1024]{1,0:T(8,128)S(1)}, f32[128,1024]{1,0:T(8,128)}, u32[]{:S(2)}) copy-start(f32[128,1024]{1,0:T(8,128)} %get-tuple-element.24.hidden_in_ref) | copy-start | bytes 1572868
  120.6 30.2 %copy-start.5 = (f32[128,512]{1,0:T(8,128)S(1)}, f32[128,512]{1,0:T(8,128)}, u32[]{:S(2)}) copy-start(f32[128,512]{1,0:T(8,128)} %get-tuple-element.25.raw_ref) | copy-start | bytes 786436
